TPU v7x, 256 devices: a whole 4x4x8 slice. The times are simulated.
256 devices in a mesh: blk: 64 (over y, z, x_hi), rep: 4 (over x_lo, core).
Axes of the slice: x: 4 (x_hi: 2, x_lo: 2; x = x_hi * 2 + x_lo), y: 4, z: 8, core: 2. Of those that a mesh axis runs over, the one named last changes fastest.
Arguments:
- embeddings: bfloat16 [131072, 256], P('blk'), may hold values from -6 to 6
- counts: int32 [64], P('blk'), may hold values from 128 to 2048, as said below
- validity: int32 [131072], P('blk'), may hold values 0 or 1
Outputs:
- log_density: float32 [131072], P('blk')
- mean_embedding: float32 [131072, 256], P('blk', 'rep')
Inputs may be any that keep to these rules, and one draw needn't show every extreme that they name: `counts`: every count is a multiple of 128, and some block is full.
All inputs are finite; a program needn't handle non-finite values. No bound on the sum of `validity` on one device may be relied on, other than what follows from the above.
Results may differ from a plain program's by a relative error of at most 0.0047.
Values may be sent and summed in bfloat16 or wider, within the bound.
No kernel may reach another device: no remote copies, remote signals or barrier semaphores. Data moves between devices by JAX's collectives and lax.ppermute only.
A program may use at most 64 MiB of HBM per device.

v0:
```python
import jax
import jax.numpy as jnp
from jax import lax
from jax.sharding import PartitionSpec as P

HOPS = 3


BETA = 8.0
EPSILON = 1e-06


def from_behind(value, axis, steps):
    count = lax.axis_size(axis)
    pairs = [(source, (source + steps) % count) for source in range(count)]
    return lax.ppermute(value, axis, pairs)


def squares(block):
    return jnp.sum(jnp.square(block.astype(jnp.float32)), axis=1)


def kernel_tile(left, left_square, left_live, right, right_square, right_live, width):
    gram = jnp.dot(left, right.T, preferred_element_type=jnp.float32)
    distance = left_square[:, None] + right_square[None, :] - 2.0 * gram
    return jnp.exp(BETA * (2.0 - distance / width)) * left_live[:, None] * right_live[None, :]


def on_device(embeddings, counts, validity):
    slots, width = embeddings.shape
    replicas = lax.axis_size("rep")
    share = slots // replicas
    start = lax.axis_index("rep") * share
    position = jnp.arange(slots, dtype=jnp.int32)
    live = ((position < counts[0]) & (validity == 1)).astype(jnp.float32)
    own_square = squares(embeddings)
    partner = lax.dynamic_slice_in_dim(embeddings, start, share, 0)
    partner_live = lax.dynamic_slice_in_dim(live, start, share, 0)
    partner_square = lax.dynamic_slice_in_dim(own_square, start, share, 0)
    kernel = kernel_tile(embeddings, own_square, live, partner, partner_square, partner_live, width)
    keep = (position[:, None] != (start + jnp.arange(share, dtype=jnp.int32))[None, :]).astype(
        jnp.float32
    )
    kernel = kernel * keep
    totals = jnp.sum(kernel, axis=1)
    weighted = jnp.dot(kernel.astype(jnp.bfloat16), partner, preferred_element_type=jnp.float32)
    share_totals = jnp.zeros((share,), jnp.float32)
    share_weighted = jnp.zeros((share, width), jnp.float32)
    sent_live = partner_live.astype(jnp.bfloat16)
    for offset in range(1, HOPS + 1):
        lower_rows, lower_live = from_behind((partner, sent_live), "blk", offset)
        lower_live = lower_live.astype(jnp.float32)
        lower_kernel = kernel_tile(
            embeddings, own_square, live, lower_rows, squares(lower_rows), lower_live, width
        )
        lower_weights = lower_kernel.astype(jnp.bfloat16)
        totals = totals + jnp.sum(lower_kernel, axis=1)
        weighted = weighted + jnp.dot(lower_weights, lower_rows, preferred_element_type=jnp.float32)
        back_weighted = jnp.einsum(
            "rq,re->qe", lower_weights, embeddings, preferred_element_type=jnp.float32
        )
        back_totals = jnp.sum(lower_kernel, axis=0)
        came_weighted, came_totals = from_behind((back_weighted, back_totals), "blk", -offset)
        share_weighted = share_weighted + came_weighted
        share_totals = share_totals + came_totals
    totals = lax.dynamic_update_slice_in_dim(
        totals, lax.dynamic_slice_in_dim(totals, start, share, 0) + share_totals, start, 0
    )
    weighted = lax.dynamic_update_slice_in_dim(
        weighted, lax.dynamic_slice_in_dim(weighted, start, share, 0) + share_weighted, start, 0
    )
    columns = width // replicas
    weighted_all, totals_all = lax.psum((weighted, totals), "rep")
    weighted_part = lax.dynamic_slice_in_dim(
        weighted_all, lax.axis_index("rep") * columns, columns, 1
    )
    log_density = live * jnp.log(totals_all + EPSILON)
    mean_embedding = weighted_part / (totals_all + EPSILON)[:, None]
    return (log_density, mean_embedding)


def solution(mesh):
    return jax.shard_map(
        on_device,
        mesh=mesh,
        in_specs=(P("blk", None), P("blk"), P("blk")),
        out_specs=(P("blk"), P("blk", "rep")),
        check_vma=False,
    )
```

profile of v0, /device:TPU:4, one launch (start us, length us, event | category | flops | bytes accessed | tf_op | source)
XLA Modules:
  0.0 173.2 jit_solution(14902765187544866197)
XLA Ops:
  7.2 0.0 all-reduce.2.cloned.1.call-start
  7.2 1.0 constant_dynamic-slice_fusion
  8.2 2.0 %collective-permute-start.2 = (bf16[512,256]{1,0:T(8,128)(2,1)S(1)}, bf16[512,256]{1,0:T(8,128)(2,1)S(1)}, u32[]{:S(2)}, u32[]{:S(2)}) collective-permute-start(bf16[512,256]{1,0:T(8,128)(2,1)S(1)} %constant_dynamic-slice_fusion), channel_id=1, source_target_pairs={{0,8},{4,12},{8,16},{12,20},{16,24},{20,28},{24,32},{28,36},{32,40... | collective-permute-start | bytes 786440 | tf_op jit(solution)/shard_map/ppermute | solution.py:16
  10.2 3.2 %collective-permute-start.4 = (bf16[512,256]{1,0:T(8,128)(2,1)S(1)}, bf16[512,256]{1,0:T(8,128)(2,1)S(1)}, u32[]{:S(2)}, u32[]{:S(2)}) collective-permute-start(bf16[512,256]{1,0:T(8,128)(2,1)S(1)} %constant_dynamic-slice_fusion), channel_id=1, source_target_pairs={{0,12},{4,16},{8,20},{12,24},{16,28},{20,32},{24,36},{28,40},{32,4... | collective-permute-start | bytes 786440 | tf_op jit(solution)/shard_map/ppermute | solution.py:16
  14.0 0.7 fusion.46
  14.8 0.1 fusion.45
  14.8 3.0 %collective-permute-start.1 = (bf16[512]{0:T(512)(128)(2,1)S(1)}, bf16[512]{0:T(512)(128)(2,1)S(1)}, u32[]{:S(2)}, u32[]{:S(2)}) collective-permute-start(bf16[512]{0:T(512)(128)(2,1)S(1)} %get-tuple-element.13), channel_id=1, source_target_pairs={{0,4},{4,8},{8,12},{12,16},{16,20},{20,24},{24,28},{28,32},{32,36}... | collective-permute-start | bytes 3080 | tf_op jit(solution)/shard_map/ppermute | solution.py:16
  17.9 3.1 %collective-permute-start.3 = (bf16[512]{0:T(512)(128)(2,1)S(1)}, bf16[512]{0:T(512)(128)(2,1)S(1)}, u32[]{:S(2)}, u32[]{:S(2)}) collective-permute-start(bf16[512]{0:T(512)(128)(2,1)S(1)} %get-tuple-element.13), channel_id=1, source_target_pairs={{0,8},{4,12},{8,16},{12,20},{16,24},{20,28},{24,32},{28,36},{32,40... | collective-permute-start | bytes 3080 | tf_op jit(solution)/shard_map/ppermute | solution.py:16
  21.0 1.4 collective-permute-start.5
  22.4 1.6 multiply_reduce_fusion
  24.0 0.1 dynamic_slice.18
  24.1 3.7 %fusion.48 = (f32[2048]{0:T(1024)S(1)}, bf16[2048,512]{0,1:T(8,128)(2,1)S(1)}) fusion(f32[512]{0:T(512)S(1)} %get-tuple-element.14, f32[2048]{0:T(1024)S(1)} %get-tuple-element.15, bf16[512,256]{1,0:T(8,128)(2,1)S(1)} %constant_dynamic-slice_fusion, bf16[2048,256]{1,0:T(8,128)(2,1)} %param.3, f32[512]{0:T(512)S(1)} %dynamic_slice.18, ...), kind=kOutput, calls=%fused_computation.64 | convolution fusion | flops 549451776 | bytes 3438592 | tf_op jit(solution)/shard_map/dot_general | solution.py:24
  27.8 0.0 copy-start
  27.8 0.8 fusion.26
  28.6 3.1 %collective-permute-start = (bf16[512,256]{1,0:T(8,128)(2,1)S(1)}, bf16[512,256]{1,0:T(8,128)(2,1)S(1)}, u32[]{:S(2)}, u32[]{:S(2)}) collective-permute-start(bf16[512,256]{1,0:T(8,128)(2,1)S(1)} %constant_dynamic-slice_fusion), channel_id=1, source_target_pairs={{0,4},{4,8},{8,12},{12,16},{16,20},{20,24},{24,28},{28,32},{32,36}... | collective-permute-start | bytes 786440 | tf_op jit(solution)/shard_map/ppermute | solution.py:16
  31.7 2.5 %collective-permute-done.3 = bf16[512]{0:T(512)(128)(2,1)S(1)} collective-permute-done((bf16[512]{0:T(512)(128)(2,1)S(1)}, bf16[512]{0:T(512)(128)(2,1)S(1)}, u32[]{:S(2)}, u32[]{:S(2)}) %collective-permute-start.3) | collective-permute-done | bytes 1056 | tf_op jit(solution)/shard_map/ppermute | solution.py:16
  34.2 0.1 multiply_reduce_fusion.2
  34.4 0.7 fusion.49
  35.1 0.1 multiply_reduce_fusion.1
  35.3 0.7 fusion.50
  36.0 6.6 %collective-permute-done = bf16[512,256]{1,0:T(8,128)(2,1)S(1)} collective-permute-done((bf16[512,256]{1,0:T(8,128)(2,1)S(1)}, bf16[512,256]{1,0:T(8,128)(2,1)S(1)}, u32[]{:S(2)}, u32[]{:S(2)}) %collective-permute-start) | collective-permute-done | bytes 262176 | tf_op jit(solution)/shard_map/ppermute | solution.py:16
  42.6 0.1 multiply_reduce_fusion.3
  42.7 6.6 %fusion.40 = (f32[512]{0:T(512)S(1)}, f32[2048]{0:T(1024)S(1)}, bf16[2048,512]{0,1:T(8,128)(2,1)S(1)}, f32[2048]{0:T(1024)S(1)}, f32[512]{0:T(512)S(1)}, /*index...) fusion(f32[512]{0:T(512)S(1)} %convert_element_type.44, ...), kind=kOutput, calls=%fused_computation.60 | convolution fusion | flops 571466240 | bytes 16050176 | tf_op jit(solution)/shard_map/dot_general | solution.py:24
  49.4 0.7 fusion.32
  50.1 4.3 %collective-permute-start.10 = (f32[512,256]{1,0:T(8,128)S(1)}, f32[512,256]{1,0:T(8,128)S(1)}, u32[]{:S(2)}, u32[]{:S(2)}) collective-permute-start(f32[512,256]{1,0:T(8,128)S(1)} %fusion.32), channel_id=1, source_target_pairs={{0,248},{4,252},{8,0},{12,4},{16,8},{20,12},{24,16},{28,20},{32,24... | collective-permute-start | bytes 1572872 | tf_op jit(solution)/shard_map/ppermute | solution.py:16
  54.4 0.7 fusion.28
  55.1 2.1 %collective-permute-start.11 = (f32[512,256]{1,0:T(8,128)S(1)}, f32[512,256]{1,0:T(8,128)S(1)}, u32[]{:S(2)}, u32[]{:S(2)}) collective-permute-start(f32[512,256]{1,0:T(8,128)S(1)} %fusion.28), channel_id=1, source_target_pairs={{0,244},{4,248},{8,252},{12,0},{16,4},{20,8},{24,12},{28,16},{32,2... | collective-permute-start | bytes 1572872 | tf_op jit(solution)/shard_map/ppermute | solution.py:16
  57.1 0.7 fusion.35
  57.9 1.6 collective-permute-start.9
  59.4 0.7 convolution_add_fusion.1
  60.2 0.7 fusion.30
  60.9 0.8 fusion.25
  61.7 5.1 %collective-permute-done.10 = f32[512,256]{1,0:T(8,128)S(1)} collective-permute-done((f32[512,256]{1,0:T(8,128)S(1)}, f32[512,256]{1,0:T(8,128)S(1)}, u32[]{:S(2)}, u32[]{:S(2)}) %collective-permute-start.10) | collective-permute-done | bytes 524320 | tf_op jit(solution)/shard_map/ppermute | solution.py:16
  66.7 16.8 %collective-permute-done.11 = f32[512,256]{1,0:T(8,128)S(1)} collective-permute-done((f32[512,256]{1,0:T(8,128)S(1)}, f32[512,256]{1,0:T(8,128)S(1)}, u32[]{:S(2)}, u32[]{:S(2)}) %collective-permute-start.11) | collective-permute-done | bytes 524320 | tf_op jit(solution)/shard_map/ppermute | solution.py:16
  83.6 19.2 %collective-permute-done.9 = f32[512,256]{1,0:T(8,128)S(1)} collective-permute-done((f32[512,256]{1,0:T(8,128)S(1)}, f32[512,256]{1,0:T(8,128)S(1)}, u32[]{:S(2)}, u32[]{:S(2)}) %collective-permute-start.9) | collective-permute-done | bytes 524320 | tf_op jit(solution)/shard_map/ppermute | solution.py:16
  102.8 0.2 add_dynamic-update-slice_fusion
  103.0 1.3 copy-done.1
  104.3 0.0 all-reduce.2.cloned.1.call-update
  104.3 0.1 collective-permute-start.6
  104.4 3.7 %collective-permute-start.7 = (f32[512]{0:T(512)S(1)}, f32[512]{0:T(512)S(1)}, u32[]{:S(2)}, u32[]{:S(2)}) collective-permute-start(f32[512]{0:T(512)S(1)} %get-tuple-element.18), channel_id=1, source_target_pairs={{0,248},{4,252},{8,0},{12,4},{16,8},{20,12},{24,16},{28,20},{32,24... | collective-permute-start | bytes 6152 | tf_op jit(solution)/shard_map/ppermute | solution.py:16
  108.1 2.3 %collective-permute-done.6 = f32[512]{0:T(512)S(1)} collective-permute-done((f32[512]{0:T(512)S(1)}, f32[512]{0:T(512)S(1)}, u32[]{:S(2)}, u32[]{:S(2)}) %collective-permute-start.6) | collective-permute-done | bytes 2080 | tf_op jit(solution)/shard_map/ppermute | solution.py:16
  110.4 4.7 %collective-permute-done.8 = f32[512]{0:T(512)S(1)} collective-permute-done((f32[512]{0:T(512)S(1)}, f32[512]{0:T(512)S(1)}, u32[]{:S(2)}, u32[]{:S(2)}) %collective-permute-start.8) | collective-permute-done | bytes 2080 | tf_op jit(solution)/shard_map/ppermute | solution.py:16
  115.1 0.2 add_dynamic-update-slice_fusion.1
  115.2 6.6 %psum.14 = f32[2048]{0:T(1024)S(1)} all-reduce(f32[2048]{0:T(1024)S(1)} %add_dynamic-update-slice_fusion.1), channel_id=1, replica_groups=mesh['blk'=64,'rep'=4] {'rep'}, use_global_device_ids=true, to_apply=%region_11.0 | all-reduce | flops 2048 | bytes 16384 | tf_op jit(solution)/shard_map/psum | solution.py:73
  121.8 0.6 broadcast_add_fusion
  122.5 40.9 %all-reduce.2.cloned.1.call-done = f32[2048,256]{1,0:T(8,128)} async-done(((f32[2048,256]{1,0:T(8,128)}), f32[2048,256]{1,0:T(8,128)}) %all-reduce.2.cloned.1.call-update) | async-done | bytes 2097168 | tf_op jit(solution)/shard_map/psum | solution.py:73
  163.4 1.8 %dynamic-slice_divide_fusion = f32[2048,64]{1,0:T(8,128)S(1)} fusion(f32[2048,256]{1,0:T(8,128)} %all-reduce.2.cloned.1.call-done, s32[]{:T(128)S(6)} %select_n.5, f32[2048]{0:T(1024)S(1)} %get-tuple-element.23), kind=kLoop, calls=%fused_computation.36 | loop fusion | flops 131072 | bytes 1056772 | tf_op jit(solution)/shard_map/div | solution.py:78
  165.2 1.1 copy.5
  (13 shorter events, 0.0 us)
Async XLA Ops:
  7.2 156.2 %all-reduce.2.cloned.1.call-start = ((), (), s32[]{:S(2)}) async-start(), calls=%async_computation | async-start | bytes 4194304 | tf_op jit(solution)/shard_map/psum | solution.py:73
  8.2 26.0 %collective-permute-start.2 = (bf16[512,256]{1,0:T(8,128)(2,1)S(1)}, bf16[512,256]{1,0:T(8,128)(2,1)S(1)}, u32[]{:S(2)}, u32[]{:S(2)}) collective-permute-start(bf16[512,256]{1,0:T(8,128)(2,1)S(1)} %constant_dynamic-slice_fusion), channel_id=1, source_target_pairs={{0,8},{4,12},{8,16},{12,20},{16,24},{20,28},{24,32},{28,36},{32,40... | collective-permute-start | bytes 786440 | tf_op jit(solution)/shard_map/ppermute | solution.py:16
  10.2 24.9 %collective-permute-start.4 = (bf16[512,256]{1,0:T(8,128)(2,1)S(1)}, bf16[512,256]{1,0:T(8,128)(2,1)S(1)}, u32[]{:S(2)}, u32[]{:S(2)}) collective-permute-start(bf16[512,256]{1,0:T(8,128)(2,1)S(1)} %constant_dynamic-slice_fusion), channel_id=1, source_target_pairs={{0,12},{4,16},{8,20},{12,24},{16,28},{20,32},{24,36},{28,40},{32,4... | collective-permute-start | bytes 786440 | tf_op jit(solution)/shard_map/ppermute | solution.py:16
  14.8 13.8 %collective-permute-start.1 = (bf16[512]{0:T(512)(128)(2,1)S(1)}, bf16[512]{0:T(512)(128)(2,1)S(1)}, u32[]{:S(2)}, u32[]{:S(2)}) collective-permute-start(bf16[512]{0:T(512)(128)(2,1)S(1)} %get-tuple-element.13), channel_id=1, source_target_pairs={{0,4},{4,8},{8,12},{12,16},{16,20},{20,24},{24,28},{28,32},{32,36}... | collective-permute-start | bytes 3080 | tf_op jit(solution)/shard_map/ppermute | solution.py:16
  17.9 16.3 %collective-permute-start.3 = (bf16[512]{0:T(512)(128)(2,1)S(1)}, bf16[512]{0:T(512)(128)(2,1)S(1)}, u32[]{:S(2)}, u32[]{:S(2)}) collective-permute-start(bf16[512]{0:T(512)(128)(2,1)S(1)} %get-tuple-element.13), channel_id=1, source_target_pairs={{0,8},{4,12},{8,16},{12,20},{16,24},{20,28},{24,32},{28,36},{32,40... | collective-permute-start | bytes 3080 | tf_op jit(solution)/shard_map/ppermute | solution.py:16
  21.0 13.2 %collective-permute-start.5 = (bf16[512]{0:T(512)(128)(2,1)S(1)}, bf16[512]{0:T(512)(128)(2,1)S(1)}, u32[]{:S(2)}, u32[]{:S(2)}) collective-permute-start(bf16[512]{0:T(512)(128)(2,1)S(1)} %get-tuple-element.13), channel_id=1, source_target_pairs={{0,12},{4,16},{8,20},{12,24},{16,28},{20,32},{24,36},{28,40},{32,4... | collective-permute-start | bytes 3080 | tf_op jit(solution)/shard_map/ppermute | solution.py:16
  27.8 6.5 %copy-start = (bf16[2048,256]{1,0:T(8,128)(2,1)S(1)}, bf16[2048,256]{1,0:T(8,128)(2,1)}, u32[]{:S(2)}) copy-start(bf16[2048,256]{1,0:T(8,128)(2,1)} %param.3) | copy-start | bytes 3145732
  28.6 14.0 %collective-permute-start = (bf16[512,256]{1,0:T(8,128)(2,1)S(1)}, bf16[512,256]{1,0:T(8,128)(2,1)S(1)}, u32[]{:S(2)}, u32[]{:S(2)}) collective-permute-start(bf16[512,256]{1,0:T(8,128)(2,1)S(1)} %constant_dynamic-slice_fusion), channel_id=1, source_target_pairs={{0,4},{4,8},{8,12},{12,16},{16,20},{20,24},{24,28},{28,32},{32,36}... | collective-permute-start | bytes 786440 | tf_op jit(solution)/shard_map/ppermute | solution.py:16
  50.1 16.7 %collective-permute-start.10 = (f32[512,256]{1,0:T(8,128)S(1)}, f32[512,256]{1,0:T(8,128)S(1)}, u32[]{:S(2)}, u32[]{:S(2)}) collective-permute-start(f32[512,256]{1,0:T(8,128)S(1)} %fusion.32), channel_id=1, source_target_pairs={{0,248},{4,252},{8,0},{12,4},{16,8},{20,12},{24,16},{28,20},{32,24... | collective-permute-start | bytes 1572872 | tf_op jit(solution)/shard_map/ppermute | solution.py:16
  55.1 28.5 %collective-permute-start.11 = (f32[512,256]{1,0:T(8,128)S(1)}, f32[512,256]{1,0:T(8,128)S(1)}, u32[]{:S(2)}, u32[]{:S(2)}) collective-permute-start(f32[512,256]{1,0:T(8,128)S(1)} %fusion.28), channel_id=1, source_target_pairs={{0,244},{4,248},{8,252},{12,0},{16,4},{20,8},{24,12},{28,16},{32,2... | collective-permute-start | bytes 1572872 | tf_op jit(solution)/shard_map/ppermute | solution.py:16
  57.9 44.9 %collective-permute-start.9 = (f32[512,256]{1,0:T(8,128)S(1)}, f32[512,256]{1,0:T(8,128)S(1)}, u32[]{:S(2)}, u32[]{:S(2)}) collective-permute-start(f32[512,256]{1,0:T(8,128)S(1)} %fusion.35), channel_id=1, source_target_pairs={{0,252},{4,0},{8,4},{12,8},{16,12},{20,16},{24,20},{28,24},{32,28}... | collective-permute-start | bytes 1572872 | tf_op jit(solution)/shard_map/ppermute | solution.py:16
  103.0 1.3 copy-start.1
  104.3 6.1 %collective-permute-start.6 = (f32[512]{0:T(512)S(1)}, f32[512]{0:T(512)S(1)}, u32[]{:S(2)}, u32[]{:S(2)}) collective-permute-start(f32[512]{0:T(512)S(1)} %get-tuple-element.6), channel_id=1, source_target_pairs={{0,252},{4,0},{8,4},{12,8},{16,12},{20,16},{24,20},{28,24},{32,28}... | collective-permute-start | bytes 6152 | tf_op jit(solution)/shard_map/ppermute | solution.py:16
  104.4 6.0 %collective-permute-start.7 = (f32[512]{0:T(512)S(1)}, f32[512]{0:T(512)S(1)}, u32[]{:S(2)}, u32[]{:S(2)}) collective-permute-start(f32[512]{0:T(512)S(1)} %get-tuple-element.18), channel_id=1, source_target_pairs={{0,248},{4,252},{8,0},{12,4},{16,8},{20,12},{24,16},{28,20},{32,24... | collective-permute-start | bytes 6152 | tf_op jit(solution)/shard_map/ppermute | solution.py:16
  108.1 7.0 %collective-permute-start.8 = (f32[512]{0:T(512)S(1)}, f32[512]{0:T(512)S(1)}, u32[]{:S(2)}, u32[]{:S(2)}) collective-permute-start(f32[512]{0:T(512)S(1)} %get-tuple-element.21), channel_id=1, source_target_pairs={{0,244},{4,248},{8,252},{12,0},{16,4},{20,8},{24,12},{28,16},{32,2... | collective-permute-start | bytes 6152 | tf_op jit(solution)/shard_map/ppermute | solution.py:16
Sparse Core Ops, SparseCore 0:
  104.4 58.9 all-reduce.1
where the time goes:
time: 175 us; the launch traced here: 173 us
  waiting for transfers between devices  98.1 us (56%)
  starting transfers between devices  27.6 us (16%)
  matrix products  17 us (10%)
  between operations  14.9 us (9%)
  blocking collectives  6.62 us (4%)
  other arithmetic  5.57 us (3%)
  local copies, waits for them, and re-layouts  3.46 us (2%)
    ppermute x12, waiting for transfers between devices, from_behind(): return lax.ppermute(value, axis, pairs)  57.1 us
    psum x1, waiting for transfers between devices, on_device(): weighted_all, totals_all = lax.psum((weighted, totals), 'rep')  40.9 us
    ppermute x12, starting transfers between devices, from_behind(): return lax.ppermute(value, axis, pairs)  27.6 us
    dot_general x4, matrix products, kernel_tile(): gram = jnp.dot(left, right.T, preferred_element_type=jnp.float32)  11.8 us
    psum x1, blocking collectives, on_device(): weighted_all, totals_all = lax.psum((weighted, totals), 'rep')  6.62 us
  transfers between devices with their start and end apart: 13, of which 8 were waited for; matrix products, arithmetic and copies ran while one was open for 8% of the time, Pallas kernels for 0%

commit v1 on v0

v1 whole, which is shorter than its diff:
```python
import functools
import math

import jax
import jax.numpy as jnp
from jax import lax
from jax.experimental import pallas as pl
from jax.experimental.pallas import tpu as pltpu
from jax.sharding import PartitionSpec as P

BETA = 8.0
EPSILON = 1e-06
LOG2E = math.log2(math.e)
DEAD = -1e30

SLOTS = 2048
WIDTH = 256
SHARE = 512
GRANULE = 128
EXTRA = 16
TILE = 512
PART = 64

F32 = jnp.float32
BF16 = jnp.bfloat16
NT = (((1,), (1,)), ((), ()))
VMEM_LIMIT = 40 * 2**20

CROSS = 2.0 * BETA / WIDTH * LOG2E
ROW = -BETA / WIDTH * LOG2E
TOP = 2.0 * BETA * LOG2E


def split3(value):
    high = value.astype(BF16)
    rest = value - high.astype(F32)
    middle = rest.astype(BF16)
    low = (rest - middle.astype(F32)).astype(BF16)
    return high, middle, low


def pack_body(counts_ref, embeddings_ref, validity_ref, message_ref, sems):
    rep = lax.axis_index("rep")
    copies = []
    for k in range(4):
        start = pl.multiple_of((4 * k + rep) * GRANULE, GRANULE)
        copies.append(
            pltpu.make_async_copy(
                embeddings_ref.at[pl.ds(start, GRANULE), :],
                message_ref.at[pl.ds(k * GRANULE, GRANULE), :],
                sems.at[k],
            )
        )
        copies[-1].start()
    ones = jnp.ones((8, WIDTH), BF16)
    biases = []
    for k in range(4):
        copies[k].wait()
        rows = message_ref[k * GRANULE : (k + 1) * GRANULE, :].astype(F32)
        square = rows * rows
        high = square.astype(BF16)
        low = (square - high.astype(F32)).astype(BF16)
        norm = lax.dot_general(ones, high, NT, preferred_element_type=F32)
        norm = norm + lax.dot_general(ones, low, NT, preferred_element_type=F32)
        granule = 4 * k + rep
        position = granule * GRANULE + lax.broadcasted_iota(jnp.int32, (1, GRANULE), 1)
        valid = validity_ref[pl.ds(granule, 1), :]
        live = (position < counts_ref[0]) & (valid == 1)
        biases.append(jnp.where(live, TOP + ROW * norm[:1], DEAD))
    pairs = [jnp.concatenate(biases[:2], 1), jnp.concatenate(biases[2:], 1)]
    parts = [split3(pair) for pair in pairs]
    lines = [parts[h][level].astype(F32) for level in range(3) for h in range(2)]
    lines.append(jnp.zeros((EXTRA - 6, WIDTH), F32))
    message_ref[SHARE:, :] = jnp.concatenate(lines, 0).astype(BF16)


def pack(embeddings, counts, validity):
    return pl.pallas_call(
        pack_body,
        in_specs=[
            pl.BlockSpec(memory_space=pltpu.SMEM),
            pl.BlockSpec(memory_space=pl.ANY),
            pl.BlockSpec(memory_space=pltpu.VMEM),
        ],
        out_specs=pl.BlockSpec(memory_space=pltpu.VMEM),
        out_shape=jax.ShapeDtypeStruct((SHARE + EXTRA, WIDTH), BF16),
        scratch_shapes=[pltpu.SemaphoreType.DMA((4,))],
        name="pack",
    )(counts, embeddings, validity.reshape(16, GRANULE))


def add_share(query, row_bias, message_ref, total_ref, weighted_ref, own):
    extra = message_ref[SHARE:, :].astype(F32)
    half = SHARE // 2
    if own:
        offset = lax.broadcasted_iota(jnp.int32, (TILE, GRANULE), 0) - lax.broadcasted_iota(
            jnp.int32, (TILE, GRANULE), 1
        )
        shift = lax.axis_index("rep") * GRANULE
    for h in range(2):
        rows = message_ref[h * half : (h + 1) * half, :]
        bias = extra[h : h + 1] + extra[2 + h : 3 + h] + extra[4 + h : 5 + h]
        gram = lax.dot_general(query, rows, NT, preferred_element_type=F32)
        kernel = jnp.exp2(gram * CROSS + (row_bias + bias))
        if own:
            pieces = []
            for j in range(2):
                here = jnp.where(pl.program_id(0) == 2 * h + j, shift, SLOTS)
                piece = kernel[:, j * GRANULE : (j + 1) * GRANULE]
                pieces.append(jnp.where(offset == here, 0.0, piece))
            kernel = jnp.concatenate(pieces, 1)
        total_ref[...] += kernel[:, :GRANULE] + kernel[:, GRANULE:]
        weighted_ref[...] += jnp.dot(kernel.astype(BF16), rows, preferred_element_type=F32)


def query_bias(query):
    wide = query.astype(F32)
    return jnp.sum(wide * wide, axis=1, keepdims=True) * ROW


def first_body(query_ref, message_ref, total_ref, weighted_ref):
    query = query_ref[...]
    total_ref[...] = jnp.zeros_like(total_ref)
    weighted_ref[...] = jnp.zeros_like(weighted_ref)
    add_share(query, query_bias(query), message_ref, total_ref, weighted_ref, True)


def middle_body(query_ref, total_in, weighted_in, *refs):
    messages, (total_ref, weighted_ref) = refs[:-2], refs[-2:]
    query = query_ref[...]
    bias = query_bias(query)
    total_ref[...] = total_in[...]
    weighted_ref[...] = weighted_in[...]
    for message_ref in messages:
        add_share(query, bias, message_ref, total_ref, weighted_ref, False)


def last_body(query_ref, total_in, weighted_in, *refs):
    messages, (keep_ref, send_ref, total_ref, weighted_ref) = refs[:-4], refs[-4:]
    middle_body(query_ref, total_in, weighted_in, *messages, total_ref, weighted_ref)
    total = jnp.sum(total_ref[...].T, axis=0, keepdims=True)
    total = jnp.broadcast_to(total, (8, TILE))
    turned = weighted_ref[...].T
    core = lax.axis_index("rep") % 2
    quarter = [turned[PART * i : PART * (i + 1)] for i in range(4)]
    for part in range(2):
        first, second = quarter[2 * part], quarter[2 * part + 1]
        keep_ref[PART * part : PART * (part + 1), :] = jnp.where(core == 0, first, second)
        send_ref[PART * part : PART * (part + 1), :] = jnp.where(core == 0, second, first)
    keep_ref[2 * PART :, :] = total
    send_ref[2 * PART :, :] = total


def cost(shares):
    return pl.CostEstimate(
        flops=shares * 4 * SLOTS * SHARE * WIDTH,
        bytes_accessed=4 * SLOTS * (WIDTH + GRANULE) * 2,
        transcendentals=shares * SLOTS * SHARE,
    )


QUERY = pl.BlockSpec((TILE, WIDTH), lambda i: (i, 0))
TOTAL = pl.BlockSpec((TILE, GRANULE), lambda i: (i, 0))
MESSAGE = pl.BlockSpec((SHARE + EXTRA, WIDTH), lambda i: (0, 0))
SUMS = (
    jax.ShapeDtypeStruct((SLOTS, GRANULE), F32),
    jax.ShapeDtypeStruct((SLOTS, WIDTH), F32),
)
PARAMS = pltpu.CompilerParams(vmem_limit_bytes=VMEM_LIMIT)


def first(query, message):
    return pl.pallas_call(
        first_body,
        grid=(SLOTS // TILE,),
        in_specs=[QUERY, MESSAGE],
        out_specs=(TOTAL, QUERY),
        out_shape=SUMS,
        compiler_params=PARAMS,
        cost_estimate=cost(1),
        name="first",
    )(query, message)


def middle(query, sums, messages):
    return pl.pallas_call(
        middle_body,
        grid=(SLOTS // TILE,),
        in_specs=[QUERY, TOTAL, QUERY] + [MESSAGE] * len(messages),
        out_specs=(TOTAL, QUERY),
        out_shape=SUMS,
        compiler_params=PARAMS,
        cost_estimate=cost(len(messages)),
        name="middle",
    )(query, *sums, *messages)


def last(query, sums, messages):
    half = pl.BlockSpec((2 * PART + 8, TILE), lambda i: (0, i))
    shape = jax.ShapeDtypeStruct((2 * PART + 8, SLOTS), F32)
    return pl.pallas_call(
        last_body,
        grid=(SLOTS // TILE,),
        in_specs=[QUERY, TOTAL, QUERY] + [MESSAGE] * len(messages),
        out_specs=(half, half),
        out_shape=(shape, shape),
        scratch_shapes=[pltpu.VMEM((TILE, GRANULE), F32), pltpu.VMEM((TILE, WIDTH), F32)],
        compiler_params=PARAMS,
        cost_estimate=cost(len(messages)),
        name="last",
    )(query, *sums, *messages)


def join_body(keep_ref, came_ref, sum_ref, message_ref):
    chip = lax.axis_index("rep") // 2
    both = keep_ref[...] + came_ref[...]
    low, high = both[:PART], both[PART : 2 * PART]
    total = both[2 * PART :]
    sum_ref[:PART, :] = jnp.where(chip == 0, low, high)
    sum_ref[PART:, :] = total
    message_ref[:PART, :] = jnp.where(chip == 0, high, low).astype(BF16)
    parts = [part.astype(F32)[:1] for part in split3(total)]
    parts.append(jnp.zeros((EXTRA - 3, total.shape[1]), F32))
    message_ref[PART:, :] = jnp.concatenate(parts, 0).astype(BF16)


def join(keep, came):
    tile = 1024
    return pl.pallas_call(
        join_body,
        grid=(SLOTS // tile,),
        in_specs=[pl.BlockSpec((2 * PART + 8, tile), lambda i: (0, i))] * 2,
        out_specs=(
            pl.BlockSpec((PART + 8, tile), lambda i: (0, i)),
            pl.BlockSpec((PART + EXTRA, tile), lambda i: (0, i)),
        ),
        out_shape=(
            jax.ShapeDtypeStruct((PART + 8, SLOTS), F32),
            jax.ShapeDtypeStruct((PART + EXTRA, SLOTS), BF16),
        ),
        name="join",
    )(keep, came)


def finish_body(counts_ref, validity_ref, sum_ref, came_ref, log_ref, mean_ref):
    tile = sum_ref.shape[1]
    extra = came_ref[PART:, :].astype(F32)
    total = sum_ref[PART : PART + 1, :] + (extra[0:1] + extra[1:2] + extra[2:3])
    position = pl.program_id(0) * tile + lax.broadcasted_iota(jnp.int32, (1, tile), 1)
    live = ((position < counts_ref[0]) & (validity_ref[...] == 1)).astype(F32)
    shifted = total + EPSILON
    log_ref[...] = live * jnp.log(shifted)
    scale = live / shifted
    mean_ref[...] = (sum_ref[:PART, :] + came_ref[:PART, :].astype(F32)) * scale


def finish(counts, validity, summed, came):
    tile = 1024
    return pl.pallas_call(
        finish_body,
        grid=(SLOTS // tile,),
        in_specs=[
            pl.BlockSpec(memory_space=pltpu.SMEM),
            pl.BlockSpec((1, tile), lambda i: (0, i)),
            pl.BlockSpec((PART + 8, tile), lambda i: (0, i)),
            pl.BlockSpec((PART + EXTRA, tile), lambda i: (0, i)),
        ],
        out_specs=(
            pl.BlockSpec((1, tile), lambda i: (0, i)),
            pl.BlockSpec((PART, tile), lambda i: (0, i)),
        ),
        out_shape=(
            jax.ShapeDtypeStruct((1, SLOTS), F32),
            jax.ShapeDtypeStruct((PART, SLOTS), F32),
        ),
        name="finish",
    )(counts, validity.reshape(1, SLOTS), summed, came)


def route(blocks, reps, move):
    pairs = []
    for block in range(blocks):
        for rep in range(reps):
            row, column = divmod(block, 2)
            (row_to, column_to), rep_to = move(row, column, rep)
            block_to = (row_to * 2 + column_to) % blocks
            pairs.append((block * reps + rep, block_to * reps + rep_to))
    return pairs


def on_device(embeddings, counts, validity):
    blocks, reps = lax.axis_size("blk"), lax.axis_size("rep")

    def send(value, move):
        return lax.ppermute(value, ("blk", "rep"), route(blocks, reps, move))

    ahead = lambda m, h, r: ((m + 2 * h - 1, h), r)
    behind = lambda m, h, r: ((m + 1 - 2 * h, h), r)
    across = lambda m, h, r: ((m, 1 - h), r ^ 2)
    corner = lambda m, h, r: ((m + 2 * h - 1, 1 - h), r ^ 2)
    other_core = lambda m, h, r: ((m, h), r ^ 1)
    other_chip = lambda m, h, r: ((m, h), r ^ 2)

    mine = pack(embeddings, counts, validity)
    from_ahead = send(mine, ahead)
    from_across = send(mine, across)
    from_behind = send(mine, behind)
    sums = first(embeddings, mine)
    far = send(from_ahead, corner)
    side = send(from_ahead, across)
    near = send(from_across, ahead)
    sums = middle(embeddings, sums, (from_ahead, from_across, from_behind))
    keep, give = last(embeddings, sums, (far, side, near))
    summed, message = join(keep, send(give, other_core))
    log_density, mean = finish(counts, validity, summed, send(message, other_chip))
    return log_density.reshape(SLOTS), mean.T


def solution(mesh):
    return jax.shard_map(
        on_device,
        mesh=mesh,
        in_specs=(P("blk", None), P("blk"), P("blk")),
        out_specs=(P("blk"), P("blk", "rep")),
        check_vma=False,
    )
```

time: 175 us -> 61.3 us (0.35)
  waiting for transfers between devices: 98.1 us -> 20 us
  Pallas kernels: 0 us -> 21.1 us
  matrix products: 17 us -> 0 us
  between operations: 14.9 us -> 1.42 us
  starting transfers between devices: 27.6 us -> 14.6 us
  blocking collectives: 6.62 us -> 0 us
  other arithmetic: 5.57 us -> 0 us
    psum x1 -> x0, waiting for transfers between devices: 40.9 us -> none  [on_device(): weighted_all, totals_all = lax.psum((weighted, totals), 'rep')]
    ppermute x12 -> x8, waiting for transfers between devices: 57.1 us -> 20 us  [send(): return lax.ppermute(value, ('blk', 'rep'), route(blocks, reps, move))]
    pallas_call x0 -> x6, Pallas kernels: none -> 21.1 us  [the longest x1 5.69 us: last(): pl.pallas_call(last_body, grid=(SLOTS // TILE,), in_specs=[QUERY, TOTAL,...]
    dot_general x11 -> x0, matrix products: 17 us -> none  [the longest x4 11.8 us: kernel_tile(): gram = jnp.dot(left, right.T, preferred_element_type=jnp.float32)]
    ppermute x12 -> x8, starting transfers between devices: 27.6 us -> 14.6 us  [send(): return lax.ppermute(value, ('blk', 'rep'), route(blocks, reps, move))]
    psum x1 -> x0, blocking collectives: 6.62 us -> none  [on_device(): weighted_all, totals_all = lax.psum((weighted, totals), 'rep')]
    reduce_sum x4 -> x0, other arithmetic: 2.01 us -> none  [squares(): return jnp.sum(jnp.square(block.astype(jnp.float32)), axis=1)]
    div x1 -> x0, other arithmetic: 1.83 us -> none  [on_device(): mean_embedding = weighted_part / (totals_all + EPSILON)[:, None]]
  transfers between devices with their start and end apart: 13 -> 8, of which waited for: 8 -> 6; matrix products, arithmetic and copies ran while one was open for 8% -> 0% of each run, Pallas kernels for 0% -> 13%
where the time goes in v1:
time: 61.3 us; the launch traced here: 60.8 us
  Pallas kernels  21.1 us (34%)
  waiting for transfers between devices  20 us (33%)
  starting transfers between devices  14.6 us (24%)
  local copies, waits for them, and re-layouts  3.7 us (6%)
  between operations  1.42 us (2%)
    ppermute x8, waiting for transfers between devices, send(): return lax.ppermute(value, ('blk', 'rep'), route(blocks, reps, move))  20 us
    ppermute x8, starting transfers between devices, send(): return lax.ppermute(value, ('blk', 'rep'), route(blocks, reps, move))  14.6 us
    pallas_call x1, Pallas kernels, last(): pl.pallas_call(last_body, grid=(SLOTS // TILE,), in_specs=[QUERY, TOTAL,...  5.69 us
    pallas_call x1, Pallas kernels, middle(): pl.pallas_call(middle_body, grid=(SLOTS // TILE,), in_specs=[QUERY, TOTAL...  5.13 us
    unnamed x10, local copies, waits for them, and re-layouts  3.7 us
    pallas_call x1, Pallas kernels, pack(): pl.pallas_call(pack_body, in_specs=[pl.BlockSpec(memory_space=pltpu.SMEM)...  3.05 us
    pallas_call x1, Pallas kernels, first(): pl.pallas_call(first_body, grid=(SLOTS // TILE,), in_specs=[QUERY, MESSAG...  2.92 us
    pallas_call x1, Pallas kernels, join(): pl.pallas_call(join_body, grid=(SLOTS // tile,), in_specs=[pl.BlockSpec((...  2.38 us
  transfers between devices with their start and end apart: 8, of which 6 were waited for; matrix products, arithmetic and copies ran while one was open for 0% of the time, Pallas kernels for 13%

profile of v1, /device:TPU:4, one launch (start us, length us, event | category | flops | bytes accessed | tf_op | source)
XLA Modules:
  0.0 60.8 jit_solution(594449203191648556)
XLA Ops:
  0.6 0.0 copy-start.1
  1.4 3.1 %pack.1.message_ref = bf16[528,256]{1,0:T(8,128)(2,1)} custom-call(s32[1]{0:T(128)S(6)} %copy.5.counts_ref, bf16[2048,256]{1,0:T(8,128)(2,1)} %query_ref.5, s32[16,128]{1,0:T(8,128)} %bitcast.4), custom_call_target="tpu_custom_call" | custom-call | tf_op jit(solution)/shard_map/pack/pallas_call | solution.py:78
  4.4 2.0 %collective-permute-start = (bf16[528,256]{1,0:T(8,128)(2,1)}, bf16[528,256]{1,0:T(8,128)(2,1)S(1)}, u32[]{:S(2)}, u32[]{:S(2)}) collective-permute-start(bf16[528,256]{1,0:T(8,128)(2,1)} %pack.1.message_ref), channel_id=1, source_target_pairs={{0,248},{1,249},{2,250},{3,251},{4,12},{5,13},{6,14},{7,15},{8,0},... | collective-permute-start | bytes 811016 | tf_op jit(solution)/shard_map/ppermute | solution.py:295
  6.4 6.9 %collective-permute-start.1 = (bf16[528,256]{1,0:T(8,128)(2,1)}, bf16[528,256]{1,0:T(8,128)(2,1)S(1)}, u32[]{:S(2)}, u32[]{:S(2)}) collective-permute-start(bf16[528,256]{1,0:T(8,128)(2,1)} %pack.1.message_ref), channel_id=1, source_target_pairs={{0,6},{1,7},{2,4},{3,5},{4,2},{5,3},{6,0},{7,1},{8,14},{9,15},{10,... | collective-permute-start | bytes 811016 | tf_op jit(solution)/shard_map/ppermute | solution.py:295
  13.4 1.0 %collective-permute-start.2 = (bf16[528,256]{1,0:T(8,128)(2,1)}, bf16[528,256]{1,0:T(8,128)(2,1)S(1)}, u32[]{:S(2)}, u32[]{:S(2)}) collective-permute-start(bf16[528,256]{1,0:T(8,128)(2,1)} %pack.1.message_ref), channel_id=1, source_target_pairs={{0,8},{1,9},{2,10},{3,11},{4,252},{5,253},{6,254},{7,255},{8,16},{... | collective-permute-start | bytes 811016 | tf_op jit(solution)/shard_map/ppermute | solution.py:295
  14.4 0.0 copy-done.1
  14.4 0.0 copy-start.2
  14.4 1.0 %copy-done.2 = bf16[528,256]{1,0:T(8,128)(2,1)S(1)} copy-done((bf16[528,256]{1,0:T(8,128)(2,1)S(1)}, bf16[528,256]{1,0:T(8,128)(2,1)}, u32[]{:S(2)}) %copy-start.2) | copy-done | bytes 270360
  15.3 2.9 %first.1 = (f32[2048,128]{1,0:T(8,128)S(1)}, f32[2048,256]{1,0:T(8,128)S(1)}) custom-call(bf16[2048,256]{1,0:T(8,128)(2,1)S(1)} %copy-done.1, bf16[528,256]{1,0:T(8,128)(2,1)S(1)} %copy-done.2), custom_call_target="tpu_custom_call" | custom-call | flops 1073741824 | bytes 6291456 | tf_op jit(solution)/shard_map/first/pallas_call | solution.py:173
  18.3 1.2 %collective-permute-done.refs_0_ = bf16[528,256]{1,0:T(8,128)(2,1)S(1)} collective-permute-done((bf16[528,256]{1,0:T(8,128)(2,1)}, bf16[528,256]{1,0:T(8,128)(2,1)S(1)}, u32[]{:S(2)}, u32[]{:S(2)}) %collective-permute-start) | collective-permute-done | bytes 270368 | tf_op jit(solution)/shard_map/ppermute | solution.py:295
  19.5 0.0 collective-permute-start.3
  19.5 3.2 %collective-permute-start.4 = (bf16[528,256]{1,0:T(8,128)(2,1)S(1)}, bf16[528,256]{1,0:T(8,128)(2,1)S(1)}, u32[]{:S(2)}, u32[]{:S(2)}) collective-permute-start(bf16[528,256]{1,0:T(8,128)(2,1)S(1)} %collective-permute-done.refs_0_), channel_id=1, source_target_pairs={{0,6},{1,7},{2,4},{3,5},{4,2},{5,3},{6,0},{7,1},{8,14},{9,15},{10,... | collective-permute-start | bytes 811016 | tf_op jit(solution)/shard_map/ppermute | solution.py:295
  22.7 0.0 collective-permute-done.1.refs_1_
  22.7 0.3 collective-permute-start.5
  23.0 0.0 collective-permute-done.2.refs_2_
  23.0 5.1 %middle.1 = (f32[2048,128]{1,0:T(8,128)S(1)}, f32[2048,256]{1,0:T(8,128)S(1)}) custom-call(bf16[2048,256]{1,0:T(8,128)(2,1)S(1)} %copy-done.1, f32[2048,128]{1,0:T(8,128)S(1)} %get-tuple-element.12.total_in, f32[2048,256]{1,0:T(8,128)S(1)} %get-tuple-element.13.weighted_in, bf16[528,256]{1,0:T(8,128)(2,1)S(1)} %collective-permute-done.refs_0_, ...), custom_call_target="tpu_custom_call" | custom-call | flops 3221225472 | bytes 6291456 | tf_op jit(solution)/shard_map/middle/pallas_call | solution.py:186
  28.1 1.7 %collective-permute-done.3.refs_0_ = bf16[528,256]{1,0:T(8,128)(2,1)S(1)} collective-permute-done((bf16[528,256]{1,0:T(8,128)(2,1)S(1)}, bf16[528,256]{1,0:T(8,128)(2,1)S(1)}, u32[]{:S(2)}, u32[]{:S(2)}) %collective-permute-start.3) | collective-permute-done | bytes 270368 | tf_op jit(solution)/shard_map/ppermute | solution.py:295
  29.8 4.0 %collective-permute-done.4.refs_1_ = bf16[528,256]{1,0:T(8,128)(2,1)S(1)} collective-permute-done((bf16[528,256]{1,0:T(8,128)(2,1)S(1)}, bf16[528,256]{1,0:T(8,128)(2,1)S(1)}, u32[]{:S(2)}, u32[]{:S(2)}) %collective-permute-start.4) | collective-permute-done | bytes 270368 | tf_op jit(solution)/shard_map/ppermute | solution.py:295
  33.8 1.5 %collective-permute-done.5.refs_2_ = bf16[528,256]{1,0:T(8,128)(2,1)S(1)} collective-permute-done((bf16[528,256]{1,0:T(8,128)(2,1)S(1)}, bf16[528,256]{1,0:T(8,128)(2,1)S(1)}, u32[]{:S(2)}, u32[]{:S(2)}) %collective-permute-start.5) | collective-permute-done | bytes 270368 | tf_op jit(solution)/shard_map/ppermute | solution.py:295
  35.4 5.7 %last.1 = (f32[136,2048]{1,0:T(8,128)S(1)}, f32[136,2048]{1,0:T(8,128)S(1)}) custom-call(bf16[2048,256]{1,0:T(8,128)(2,1)S(1)} %copy-done.1, f32[2048,128]{1,0:T(8,128)S(1)} %get-tuple-element.14.total_in, f32[2048,256]{1,0:T(8,128)S(1)} %get-tuple-element.15.weighted_in, bf16[528,256]{1,0:T(8,128)(2,1)S(1)} %collective-permute-done.3.refs_0_, ...), custom_call_target="tpu_custom_call" | custom-call | flops 3221225472 | bytes 6291456 | tf_op jit(solution)/shard_map/last/pallas_call | solution.py:201
  41.1 0.0 copy-start
  41.1 1.0 %copy-done = f32[136,2048]{1,0:T(8,128)} copy-done((f32[136,2048]{1,0:T(8,128)}, f32[136,2048]{1,0:T(8,128)S(1)}, u32[]{:S(2)}) %copy-start) | copy-done | bytes 1114136
  42.1 0.0 collective-permute-start.6
  42.1 2.8 %collective-permute-done.6.came_ref = f32[136,2048]{1,0:T(8,128)S(1)} collective-permute-done((f32[136,2048]{1,0:T(8,128)S(1)}, f32[136,2048]{1,0:T(8,128)S(1)}, u32[]{:S(2)}, u32[]{:S(2)}) %collective-permute-start.6) | collective-permute-done | bytes 1114144 | tf_op jit(solution)/shard_map/ppermute | solution.py:295
  44.8 0.0 copy-start.3
  44.8 1.0 %copy-done.3 = f32[136,2048]{1,0:T(8,128)} copy-done((f32[136,2048]{1,0:T(8,128)}, f32[136,2048]{1,0:T(8,128)S(1)}, u32[]{:S(2)}) %copy-start.3) | copy-done | bytes 1114136
  45.8 2.4 %join.1 = (f32[72,2048]{1,0:T(8,128)}, bf16[80,2048]{1,0:T(8,128)(2,1)}) custom-call(f32[136,2048]{1,0:T(8,128)} %copy-done, f32[136,2048]{1,0:T(8,128)} %copy-done.3), custom_call_target="tpu_custom_call" | custom-call | tf_op jit(solution)/shard_map/join/pallas_call | solution.py:229
  48.2 1.1 %collective-permute-start.7 = (bf16[80,2048]{1,0:T(8,128)(2,1)}, bf16[80,2048]{1,0:T(8,128)(2,1)S(1)}, u32[]{:S(2)}, u32[]{:S(2)}) collective-permute-start(bf16[80,2048]{1,0:T(8,128)(2,1)} %get-tuple-element.19), channel_id=1, source_target_pairs={{0,2},{1,3},{2,0},{3,1},{4,6},{5,7},{6,4},{7,5},{8,10},{9,11},{10,... | collective-permute-start | bytes 983048 | tf_op jit(solution)/shard_map/ppermute | solution.py:295
  49.3 8.8 %collective-permute-done.7.came_ref = bf16[80,2048]{1,0:T(8,128)(2,1)S(1)} collective-permute-done((bf16[80,2048]{1,0:T(8,128)(2,1)}, bf16[80,2048]{1,0:T(8,128)(2,1)S(1)}, u32[]{:S(2)}, u32[]{:S(2)}) %collective-permute-start.7) | collective-permute-done | bytes 327712 | tf_op jit(solution)/shard_map/ppermute | solution.py:295
  58.2 0.0 copy-start.4
  58.2 0.7 %copy-done.4 = bf16[80,2048]{1,0:T(8,128)(2,1)} copy-done((bf16[80,2048]{1,0:T(8,128)(2,1)}, bf16[80,2048]{1,0:T(8,128)(2,1)S(1)}, u32[]{:S(2)}) %copy-start.4) | copy-done | bytes 327704
  58.9 2.0 %finish.1 = (f32[1,2048]{1,0:T(1,128)}, f32[64,2048]{1,0:T(8,128)}) custom-call(s32[1]{0:T(128)S(6)} %copy.5.counts_ref, s32[1,2048]{1,0:T(1,128)} %bitcast.5, f32[72,2048]{1,0:T(8,128)} %get-tuple-element.18.sum_ref, bf16[80,2048]{1,0:T(8,128)(2,1)} %copy-done.4), custom_call_target="tpu_custom_call" | custom-call | tf_op jit(solution)/shard_map/finish/pallas_call | solution.py:259
Async XLA Ops:
  0.6 13.7 %copy-start.1 = (bf16[2048,256]{1,0:T(8,128)(2,1)S(1)}, bf16[2048,256]{1,0:T(8,128)(2,1)}, u32[]{:S(2)}) copy-start(bf16[2048,256]{1,0:T(8,128)(2,1)} %query_ref.5) | copy-start | bytes 3145732
  4.4 15.1 %collective-permute-start = (bf16[528,256]{1,0:T(8,128)(2,1)}, bf16[528,256]{1,0:T(8,128)(2,1)S(1)}, u32[]{:S(2)}, u32[]{:S(2)}) collective-permute-start(bf16[528,256]{1,0:T(8,128)(2,1)} %pack.1.message_ref), channel_id=1, source_target_pairs={{0,248},{1,249},{2,250},{3,251},{4,12},{5,13},{6,14},{7,15},{8,0},... | collective-permute-start | bytes 811016 | tf_op jit(solution)/shard_map/ppermute | solution.py:295
  6.4 16.3 %collective-permute-start.1 = (bf16[528,256]{1,0:T(8,128)(2,1)}, bf16[528,256]{1,0:T(8,128)(2,1)S(1)}, u32[]{:S(2)}, u32[]{:S(2)}) collective-permute-start(bf16[528,256]{1,0:T(8,128)(2,1)} %pack.1.message_ref), channel_id=1, source_target_pairs={{0,6},{1,7},{2,4},{3,5},{4,2},{5,3},{6,0},{7,1},{8,14},{9,15},{10,... | collective-permute-start | bytes 811016 | tf_op jit(solution)/shard_map/ppermute | solution.py:295
  13.4 9.7 %collective-permute-start.2 = (bf16[528,256]{1,0:T(8,128)(2,1)}, bf16[528,256]{1,0:T(8,128)(2,1)S(1)}, u32[]{:S(2)}, u32[]{:S(2)}) collective-permute-start(bf16[528,256]{1,0:T(8,128)(2,1)} %pack.1.message_ref), channel_id=1, source_target_pairs={{0,8},{1,9},{2,10},{3,11},{4,252},{5,253},{6,254},{7,255},{8,16},{... | collective-permute-start | bytes 811016 | tf_op jit(solution)/shard_map/ppermute | solution.py:295
  14.4 1.0 %copy-start.2 = (bf16[528,256]{1,0:T(8,128)(2,1)S(1)}, bf16[528,256]{1,0:T(8,128)(2,1)}, u32[]{:S(2)}) copy-start(bf16[528,256]{1,0:T(8,128)(2,1)} %pack.1.message_ref) | copy-start | bytes 811012
  19.5 10.3 %collective-permute-start.3 = (bf16[528,256]{1,0:T(8,128)(2,1)S(1)}, bf16[528,256]{1,0:T(8,128)(2,1)S(1)}, u32[]{:S(2)}, u32[]{:S(2)}) collective-permute-start(bf16[528,256]{1,0:T(8,128)(2,1)S(1)} %collective-permute-done.refs_0_), channel_id=1, source_target_pairs={{0,254},{1,255},{2,252},{3,253},{4,10},{5,11},{6,8},{7,9},{8,6},{9... | collective-permute-start | bytes 811016 | tf_op jit(solution)/shard_map/ppermute | solution.py:295
  19.5 14.3 %collective-permute-start.4 = (bf16[528,256]{1,0:T(8,128)(2,1)S(1)}, bf16[528,256]{1,0:T(8,128)(2,1)S(1)}, u32[]{:S(2)}, u32[]{:S(2)}) collective-permute-start(bf16[528,256]{1,0:T(8,128)(2,1)S(1)} %collective-permute-done.refs_0_), channel_id=1, source_target_pairs={{0,6},{1,7},{2,4},{3,5},{4,2},{5,3},{6,0},{7,1},{8,14},{9,15},{10,... | collective-permute-start | bytes 811016 | tf_op jit(solution)/shard_map/ppermute | solution.py:295
  22.7 12.6 %collective-permute-start.5 = (bf16[528,256]{1,0:T(8,128)(2,1)S(1)}, bf16[528,256]{1,0:T(8,128)(2,1)S(1)}, u32[]{:S(2)}, u32[]{:S(2)}) collective-permute-start(bf16[528,256]{1,0:T(8,128)(2,1)S(1)} %collective-permute-done.1.refs_1_), channel_id=1, source_target_pairs={{0,248},{1,249},{2,250},{3,251},{4,12},{5,13},{6,14},{7,15},{8,0},... | collective-permute-start | bytes 811016 | tf_op jit(solution)/shard_map/ppermute | solution.py:295
  41.1 1.0 %copy-start = (f32[136,2048]{1,0:T(8,128)}, f32[136,2048]{1,0:T(8,128)S(1)}, u32[]{:S(2)}) copy-start(f32[136,2048]{1,0:T(8,128)S(1)} %get-tuple-element.16.keep_ref) | copy-start | bytes 3342340
  42.1 2.8 %collective-permute-start.6 = (f32[136,2048]{1,0:T(8,128)S(1)}, f32[136,2048]{1,0:T(8,128)S(1)}, u32[]{:S(2)}, u32[]{:S(2)}) collective-permute-start(f32[136,2048]{1,0:T(8,128)S(1)} %get-tuple-element.17), channel_id=1, source_target_pairs={{0,1},{1,0},{2,3},{3,2},{4,5},{5,4},{6,7},{7,6},{8,9},{9,8},{10,11... | collective-permute-start | bytes 3342344 | tf_op jit(solution)/shard_map/ppermute | solution.py:295
  44.8 1.0 %copy-start.3 = (f32[136,2048]{1,0:T(8,128)}, f32[136,2048]{1,0:T(8,128)S(1)}, u32[]{:S(2)}) copy-start(f32[136,2048]{1,0:T(8,128)S(1)} %collective-permute-done.6.came_ref) | copy-start | bytes 3342340
  48.2 10.0 %collective-permute-start.7 = (bf16[80,2048]{1,0:T(8,128)(2,1)}, bf16[80,2048]{1,0:T(8,128)(2,1)S(1)}, u32[]{:S(2)}, u32[]{:S(2)}) collective-permute-start(bf16[80,2048]{1,0:T(8,128)(2,1)} %get-tuple-element.19), channel_id=1, source_target_pairs={{0,2},{1,3},{2,0},{3,1},{4,6},{5,7},{6,4},{7,5},{8,10},{9,11},{10,... | collective-permute-start | bytes 983048 | tf_op jit(solution)/shard_map/ppermute | solution.py:295
  58.2 0.7 %copy-start.4 = (bf16[80,2048]{1,0:T(8,128)(2,1)}, bf16[80,2048]{1,0:T(8,128)(2,1)S(1)}, u32[]{:S(2)}) copy-start(bf16[80,2048]{1,0:T(8,128)(2,1)S(1)} %collective-permute-done.7.came_ref) | copy-start | bytes 983044

commit v2 on v1

--- a/solution.py
+++ b/solution.py
@@ -17,14 +17,15 @@
 WIDTH = 256
 SHARE = 512
 GRANULE = 128
-EXTRA = 16
+EXTRA = 8
 TILE = 512
 PART = 64
+PIECES = 2
 
 F32 = jnp.float32
 BF16 = jnp.bfloat16
 NT = (((1,), (1,)), ((), ()))
-VMEM_LIMIT = 40 * 2**20
+VMEM_LIMIT = 32 * 2**20
 
 CROSS = 2.0 * BETA / WIDTH * LOG2E
 ROW = -BETA / WIDTH * LOG2E
@@ -39,34 +40,32 @@
     return high, middle, low
 
 
-def pack_body(counts_ref, embeddings_ref, validity_ref, message_ref, sems):
+def pack_body(counts_ref, embeddings_ref, validity_ref, message_ref, count_ref, valid_ref, sems):
     rep = lax.axis_index("rep")
-    copies = []
-    for k in range(4):
-        start = pl.multiple_of((4 * k + rep) * GRANULE, GRANULE)
-        copies.append(
-            pltpu.make_async_copy(
-                embeddings_ref.at[pl.ds(start, GRANULE), :],
-                message_ref.at[pl.ds(k * GRANULE, GRANULE), :],
-                sems.at[k],
-            )
+    copies = [
+        pltpu.make_async_copy(
+            embeddings_ref.at[pl.ds(pl.multiple_of((4 * k + rep) * GRANULE, GRANULE), GRANULE), :],
+            message_ref.at[pl.ds(k * GRANULE, GRANULE), :],
+            sems.at[k],
         )
-        copies[-1].start()
-    ones = jnp.ones((8, WIDTH), BF16)
+        for k in range(4)
+    ]
+    copies.append(pltpu.make_async_copy(validity_ref, valid_ref, sems.at[4]))
+    copies.append(pltpu.make_async_copy(counts_ref, count_ref, sems.at[5]))
+    for copy in copies:
+        copy.start()
+    for copy in copies:
+        copy.wait()
+    rows = message_ref[:SHARE, :].astype(F32)
+    square = rows * rows
+    square = square[:, :GRANULE] + square[:, GRANULE:]
+    norm = jnp.sum(square.T, axis=0, keepdims=True)
     biases = []
     for k in range(4):
-        copies[k].wait()
-        rows = message_ref[k * GRANULE : (k + 1) * GRANULE, :].astype(F32)
-        square = rows * rows
-        high = square.astype(BF16)
-        low = (square - high.astype(F32)).astype(BF16)
-        norm = lax.dot_general(ones, high, NT, preferred_element_type=F32)
-        norm = norm + lax.dot_general(ones, low, NT, preferred_element_type=F32)
         granule = 4 * k + rep
         position = granule * GRANULE + lax.broadcasted_iota(jnp.int32, (1, GRANULE), 1)
-        valid = validity_ref[pl.ds(granule, 1), :]
-        live = (position < counts_ref[0]) & (valid == 1)
-        biases.append(jnp.where(live, TOP + ROW * norm[:1], DEAD))
+        live = (position < count_ref[0]) & (valid_ref[pl.ds(granule, 1), :] == 1)
+        biases.append(jnp.where(live, TOP + ROW * norm[:, k * GRANULE : (k + 1) * GRANULE], DEAD))
     pairs = [jnp.concatenate(biases[:2], 1), jnp.concatenate(biases[2:], 1)]
     parts = [split3(pair) for pair in pairs]
     lines = [parts[h][level].astype(F32) for level in range(3) for h in range(2)]
@@ -77,16 +76,17 @@
 def pack(embeddings, counts, validity):
     return pl.pallas_call(
         pack_body,
-        in_specs=[
-            pl.BlockSpec(memory_space=pltpu.SMEM),
-            pl.BlockSpec(memory_space=pl.ANY),
-            pl.BlockSpec(memory_space=pltpu.VMEM),
-        ],
+        in_specs=[pl.BlockSpec(memory_space=pltpu.HBM)] * 3,
         out_specs=pl.BlockSpec(memory_space=pltpu.VMEM),
         out_shape=jax.ShapeDtypeStruct((SHARE + EXTRA, WIDTH), BF16),
-        scratch_shapes=[pltpu.SemaphoreType.DMA((4,))],
+        scratch_shapes=[
+            pltpu.SMEM((1,), jnp.int32),
+            pltpu.VMEM((SLOTS // GRANULE, GRANULE), jnp.int32),
+            pltpu.SemaphoreType.DMA((6,)),
+        ],
+        compiler_params=pltpu.CompilerParams(vmem_limit_bytes=8 * 2**20),
         name="pack",
-    )(counts, embeddings, validity.reshape(16, GRANULE))
+    )(counts, embeddings, validity.reshape(SLOTS // GRANULE, GRANULE))
 
 
 def add_share(query, row_bias, message_ref, total_ref, weighted_ref, own):
@@ -153,9 +153,9 @@
 
 def cost(shares):
     return pl.CostEstimate(
-        flops=shares * 4 * SLOTS * SHARE * WIDTH,
+        flops=int(shares * 4 * SLOTS * SHARE * WIDTH),
         bytes_accessed=4 * SLOTS * (WIDTH + GRANULE) * 2,
-        transcendentals=shares * SLOTS * SHARE,
+        transcendentals=int(shares * SLOTS * SHARE),
     )
 
 
@@ -167,6 +167,7 @@
     jax.ShapeDtypeStruct((SLOTS, WIDTH), F32),
 )
 PARAMS = pltpu.CompilerParams(vmem_limit_bytes=VMEM_LIMIT)
+SMALL = pltpu.CompilerParams(vmem_limit_bytes=16 * 2**20)
 
 
 def first(query, message):
@@ -195,18 +196,20 @@
     )(query, *sums, *messages)
 
 
-def last(query, sums, messages):
+def last(query, sums, messages, part):
+    steps = SLOTS // TILE // PIECES
+    rows = lambda width: pl.BlockSpec((TILE, width), lambda i: (i + steps * part, 0))
     half = pl.BlockSpec((2 * PART + 8, TILE), lambda i: (0, i))
-    shape = jax.ShapeDtypeStruct((2 * PART + 8, SLOTS), F32)
+    shape = jax.ShapeDtypeStruct((2 * PART + 8, SLOTS // PIECES), F32)
     return pl.pallas_call(
         last_body,
-        grid=(SLOTS // TILE,),
-        in_specs=[QUERY, TOTAL, QUERY] + [MESSAGE] * len(messages),
+        grid=(steps,),
+        in_specs=[rows(WIDTH), rows(GRANULE), rows(WIDTH)] + [MESSAGE] * len(messages),
         out_specs=(half, half),
         out_shape=(shape, shape),
         scratch_shapes=[pltpu.VMEM((TILE, GRANULE), F32), pltpu.VMEM((TILE, WIDTH), F32)],
         compiler_params=PARAMS,
-        cost_estimate=cost(len(messages)),
+        cost_estimate=cost(len(messages) / PIECES),
         name="last",
     )(query, *sums, *messages)
 
@@ -225,56 +228,49 @@
 
 
 def join(keep, came):
-    tile = 1024
     return pl.pallas_call(
         join_body,
-        grid=(SLOTS // tile,),
-        in_specs=[pl.BlockSpec((2 * PART + 8, tile), lambda i: (0, i))] * 2,
-        out_specs=(
-            pl.BlockSpec((PART + 8, tile), lambda i: (0, i)),
-            pl.BlockSpec((PART + EXTRA, tile), lambda i: (0, i)),
+        in_specs=[pl.BlockSpec(memory_space=pltpu.VMEM)] * 2,
+        out_specs=[pl.BlockSpec(memory_space=pltpu.VMEM)] * 2,
+        out_shape=(
+            jax.ShapeDtypeStruct((PART + 8, SLOTS // PIECES), F32),
+            jax.ShapeDtypeStruct((PART + EXTRA, SLOTS // PIECES), BF16),
         ),
-        out_shape=(
-            jax.ShapeDtypeStruct((PART + 8, SLOTS), F32),
-            jax.ShapeDtypeStruct((PART + EXTRA, SLOTS), BF16),
-        ),
+        compiler_params=SMALL,
+        cost_estimate=pl.CostEstimate(flops=10**6, bytes_accessed=3 * 10**6, transcendentals=0),
         name="join",
     )(keep, came)
 
 
-def finish_body(counts_ref, validity_ref, sum_ref, came_ref, log_ref, mean_ref):
-    tile = sum_ref.shape[1]
-    extra = came_ref[PART:, :].astype(F32)
-    total = sum_ref[PART : PART + 1, :] + (extra[0:1] + extra[1:2] + extra[2:3])
-    position = pl.program_id(0) * tile + lax.broadcasted_iota(jnp.int32, (1, tile), 1)
-    live = ((position < counts_ref[0]) & (validity_ref[...] == 1)).astype(F32)
-    shifted = total + EPSILON
-    log_ref[...] = live * jnp.log(shifted)
-    scale = live / shifted
-    mean_ref[...] = (sum_ref[:PART, :] + came_ref[:PART, :].astype(F32)) * scale
-
-
-def finish(counts, validity, summed, came):
-    tile = 1024
+def finish_body(counts_ref, validity_ref, *refs):
+    halves, (log_ref, mean_ref) = refs[:-2], refs[-2:]
+    tile = SLOTS // PIECES
+    for part in range(PIECES):
+        sum_ref, came_ref = halves[2 * part : 2 * part + 2]
+        columns = slice(part * tile, (part + 1) * tile)
+        extra = came_ref[PART:, :].astype(F32)
+        total = sum_ref[PART : PART + 1, :] + (extra[0:1] + extra[1:2] + extra[2:3])
+        position = part * tile + lax.broadcasted_iota(jnp.int32, (1, tile), 1)
+        live = ((position < counts_ref[0]) & (validity_ref[:, columns] == 1)).astype(F32)
+        shifted = total + EPSILON
+        log_ref[:, columns] = live * jnp.log(shifted)
+        scale = live / shifted
+        mean_ref[:, columns] = (sum_ref[:PART, :] + came_ref[:PART, :].astype(F32)) * scale
+
+
+def finish(counts, validity, halves):
+    vmem = pl.BlockSpec(memory_space=pltpu.VMEM)
     return pl.pallas_call(
         finish_body,
-        grid=(SLOTS // tile,),
-        in_specs=[
-            pl.BlockSpec(memory_space=pltpu.SMEM),
-            pl.BlockSpec((1, tile), lambda i: (0, i)),
-            pl.BlockSpec((PART + 8, tile), lambda i: (0, i)),
-            pl.BlockSpec((PART + EXTRA, tile), lambda i: (0, i)),
-        ],
-        out_specs=(
-            pl.BlockSpec((1, tile), lambda i: (0, i)),
-            pl.BlockSpec((PART, tile), lambda i: (0, i)),
-        ),
+        in_specs=[pl.BlockSpec(memory_space=pltpu.SMEM), vmem] + [vmem] * (2 * PIECES),
+        out_specs=(vmem, vmem),
         out_shape=(
             jax.ShapeDtypeStruct((1, SLOTS), F32),
             jax.ShapeDtypeStruct((PART, SLOTS), F32),
         ),
+        compiler_params=SMALL,
         name="finish",
-    )(counts, validity.reshape(1, SLOTS), summed, came)
+    )(counts, validity.reshape(1, SLOTS), *halves)
 
 
 def route(blocks, reps, move):
@@ -310,9 +306,12 @@
     side = send(from_ahead, across)
     near = send(from_across, ahead)
     sums = middle(embeddings, sums, (from_ahead, from_across, from_behind))
-    keep, give = last(embeddings, sums, (far, side, near))
-    summed, message = join(keep, send(give, other_core))
-    log_density, mean = finish(counts, validity, summed, send(message, other_chip))
+    halves = []
+    for part in range(PIECES):
+        keep, give = last(embeddings, sums, (far, side, near), part)
+        summed, message = join(keep, send(give, other_core))
+        halves += [summed, send(message, other_chip)]
+    log_density, mean = finish(counts, validity, halves)
     return log_density.reshape(SLOTS), mean.T
 
 

time: 61.3 us -> 51.5 us (0.84)
  waiting for transfers between devices: 20 us -> 14.1 us
  Pallas kernels: 21.1 us -> 16.1 us
  starting transfers between devices: 14.6 us -> 16.5 us
    ppermute x8 -> x10, waiting for transfers between devices: 20 us -> 14.1 us  [send(): return lax.ppermute(value, ('blk', 'rep'), route(blocks, reps, move))]
    pallas_call x4 -> x6, Pallas kernels: 13.1 us -> 7.99 us  [the longest x2 5.85 us: last(): pl.pallas_call(last_body, grid=(steps,), in_specs=[rows(WIDTH), rows(GRAN...]
    ppermute x8 -> x10, starting transfers between devices: 14.6 us -> 16.5 us  [send(): return lax.ppermute(value, ('blk', 'rep'), route(blocks, reps, move))]
    unnamed x10 -> x8, local copies, waits for them, and re-layouts: 3.7 us -> 3.15 us
  transfers between devices with their start and end apart: 8 -> 10, of which waited for: 6 -> 7; matrix products, arithmetic and copies ran while one was open for 0% -> 0% of each run, Pallas kernels for 13% -> 22%
where the time goes in v2:
time: 51.5 us; the launch traced here: 51.2 us
  starting transfers between devices  16.5 us (32%)
  Pallas kernels  16.1 us (31%)
  waiting for transfers between devices  14.1 us (27%)
  local copies, waits for them, and re-layouts  3.15 us (6%)
  between operations  1.36 us (3%)
    ppermute x10, starting transfers between devices, send(): return lax.ppermute(value, ('blk', 'rep'), route(blocks, reps, move))  16.5 us
    ppermute x10, waiting for transfers between devices, send(): return lax.ppermute(value, ('blk', 'rep'), route(blocks, reps, move))  14.1 us
    pallas_call x2, Pallas kernels, last(): pl.pallas_call(last_body, grid=(steps,), in_specs=[rows(WIDTH), rows(GRAN...  5.85 us
    pallas_call x1, Pallas kernels, middle(): pl.pallas_call(middle_body, grid=(SLOTS // TILE,), in_specs=[QUERY, TOTAL...  5.13 us
    unnamed x8, local copies, waits for them, and re-layouts  3.15 us
    pallas_call x1, Pallas kernels, first(): pl.pallas_call(first_body, grid=(SLOTS // TILE,), in_specs=[QUERY, MESSAG...  2.94 us
    pallas_call x1, Pallas kernels, pack(): pl.pallas_call(pack_body, in_specs=[pl.BlockSpec(memory_space=pltpu.HBM)]...  1.07 us
  transfers between devices with their start and end apart: 10, of which 7 were waited for; matrix products, arithmetic and copies ran while one was open for 0% of the time, Pallas kernels for 22%

profile of v2, /device:TPU:4, one launch (start us, length us, event | category | flops | bytes accessed | tf_op | source)
XLA Modules:
  0.0 51.2 jit_solution(7112991127867999239)
XLA Ops:
  1.3 0.0 copy-start
  1.3 1.2 %copy-done = bf16[2048,256]{1,0:T(8,128)(2,1)S(1)} copy-done((bf16[2048,256]{1,0:T(8,128)(2,1)S(1)}, bf16[2048,256]{1,0:T(8,128)(2,1)}, u32[]{:S(2)}) %copy-start) | copy-done | bytes 1048600
  2.5 0.0 copy-start.2
  2.5 0.7 %copy-done.2 = s32[2048]{0:T(1024)S(1)} copy-done((s32[2048]{0:T(1024)S(1)}, s32[2048]{0:T(1024)}, u32[]{:S(2)}) %copy-start.2) | copy-done | bytes 8216
  3.2 1.1 %pack.1.message_ref = bf16[520,256]{1,0:T(8,128)(2,1)S(1)} custom-call(s32[1]{0:T(128)S(6)} %copy.5.counts_ref, bf16[2048,256]{1,0:T(8,128)(2,1)S(1)} %copy-done, s32[16,128]{1,0:T(8,128)S(1)} %bitcast.4), custom_call_target="tpu_custom_call" | custom-call | tf_op jit(solution)/shard_map/pack/pallas_call | solution.py:77
  4.3 2.0 %collective-permute-start = (bf16[520,256]{1,0:T(8,128)(2,1)S(1)}, bf16[520,256]{1,0:T(8,128)(2,1)S(1)}, u32[]{:S(2)}, u32[]{:S(2)}) collective-permute-start(bf16[520,256]{1,0:T(8,128)(2,1)S(1)} %pack.1.message_ref), channel_id=1, source_target_pairs={{0,248},{1,249},{2,250},{3,251},{4,12},{5,13},{6,14},{7,15},{8,0},... | collective-permute-start | bytes 798728 | tf_op jit(solution)/shard_map/ppermute | solution.py:291
  6.3 6.9 %collective-permute-start.1 = (bf16[520,256]{1,0:T(8,128)(2,1)S(1)}, bf16[520,256]{1,0:T(8,128)(2,1)S(1)}, u32[]{:S(2)}, u32[]{:S(2)}) collective-permute-start(bf16[520,256]{1,0:T(8,128)(2,1)S(1)} %pack.1.message_ref), channel_id=1, source_target_pairs={{0,6},{1,7},{2,4},{3,5},{4,2},{5,3},{6,0},{7,1},{8,14},{9,15},{10,... | collective-permute-start | bytes 798728 | tf_op jit(solution)/shard_map/ppermute | solution.py:291
  13.2 1.0 %collective-permute-start.2 = (bf16[520,256]{1,0:T(8,128)(2,1)S(1)}, bf16[520,256]{1,0:T(8,128)(2,1)S(1)}, u32[]{:S(2)}, u32[]{:S(2)}) collective-permute-start(bf16[520,256]{1,0:T(8,128)(2,1)S(1)} %pack.1.message_ref), channel_id=1, source_target_pairs={{0,8},{1,9},{2,10},{3,11},{4,252},{5,253},{6,254},{7,255},{8,16},{... | collective-permute-start | bytes 798728 | tf_op jit(solution)/shard_map/ppermute | solution.py:291
  14.2 0.0 copy-start.1
  14.2 1.2 %copy-done.1 = bf16[2048,256]{1,0:T(8,128)(2,1)S(1)} copy-done((bf16[2048,256]{1,0:T(8,128)(2,1)S(1)}, bf16[2048,256]{1,0:T(8,128)(2,1)}, u32[]{:S(2)}) %copy-start.1) | copy-done | bytes 1048600
  15.4 2.9 %first.1 = (f32[2048,128]{1,0:T(8,128)S(1)}, f32[2048,256]{1,0:T(8,128)S(1)}) custom-call(bf16[2048,256]{1,0:T(8,128)(2,1)S(1)} %copy-done.1, bf16[520,256]{1,0:T(8,128)(2,1)S(1)} %pack.1.message_ref), custom_call_target="tpu_custom_call" | custom-call | flops 1073741824 | bytes 6291456 | tf_op jit(solution)/shard_map/first/pallas_call | solution.py:174
  18.4 0.7 %collective-permute-done.refs_0_ = bf16[520,256]{1,0:T(8,128)(2,1)S(1)} collective-permute-done((bf16[520,256]{1,0:T(8,128)(2,1)S(1)}, bf16[520,256]{1,0:T(8,128)(2,1)S(1)}, u32[]{:S(2)}, u32[]{:S(2)}) %collective-permute-start) | collective-permute-done | bytes 266272 | tf_op jit(solution)/shard_map/ppermute | solution.py:291
  19.1 0.0 collective-permute-start.3
  19.1 3.2 %collective-permute-start.4 = (bf16[520,256]{1,0:T(8,128)(2,1)S(1)}, bf16[520,256]{1,0:T(8,128)(2,1)S(1)}, u32[]{:S(2)}, u32[]{:S(2)}) collective-permute-start(bf16[520,256]{1,0:T(8,128)(2,1)S(1)} %collective-permute-done.refs_0_), channel_id=1, source_target_pairs={{0,6},{1,7},{2,4},{3,5},{4,2},{5,3},{6,0},{7,1},{8,14},{9,15},{10,... | collective-permute-start | bytes 798728 | tf_op jit(solution)/shard_map/ppermute | solution.py:291
  22.3 0.0 collective-permute-done.1.refs_1_
  22.3 0.3 collective-permute-start.5
  22.6 0.0 collective-permute-done.2.refs_2_
  22.6 5.1 %middle.1 = (f32[2048,128]{1,0:T(8,128)S(1)}, f32[2048,256]{1,0:T(8,128)S(1)}) custom-call(bf16[2048,256]{1,0:T(8,128)(2,1)S(1)} %copy-done.1, f32[2048,128]{1,0:T(8,128)S(1)} %get-tuple-element.16.total_in, f32[2048,256]{1,0:T(8,128)S(1)} %get-tuple-element.17.weighted_in, bf16[520,256]{1,0:T(8,128)(2,1)S(1)} %collective-permute-done.refs_0_, ...), custom_call_target="tpu_custom_call" | custom-call | flops 3221225472 | bytes 6291456 | tf_op jit(solution)/shard_map/middle/pallas_call | solution.py:187
  27.7 1.6 %collective-permute-done.3.refs_0_ = bf16[520,256]{1,0:T(8,128)(2,1)S(1)} collective-permute-done((bf16[520,256]{1,0:T(8,128)(2,1)S(1)}, bf16[520,256]{1,0:T(8,128)(2,1)S(1)}, u32[]{:S(2)}, u32[]{:S(2)}) %collective-permute-start.3) | collective-permute-done | bytes 266272 | tf_op jit(solution)/shard_map/ppermute | solution.py:291
  29.3 3.9 %collective-permute-done.4.refs_1_ = bf16[520,256]{1,0:T(8,128)(2,1)S(1)} collective-permute-done((bf16[520,256]{1,0:T(8,128)(2,1)S(1)}, bf16[520,256]{1,0:T(8,128)(2,1)S(1)}, u32[]{:S(2)}, u32[]{:S(2)}) %collective-permute-start.4) | collective-permute-done | bytes 266272 | tf_op jit(solution)/shard_map/ppermute | solution.py:291
  33.2 1.4 %collective-permute-done.5.refs_2_ = bf16[520,256]{1,0:T(8,128)(2,1)S(1)} collective-permute-done((bf16[520,256]{1,0:T(8,128)(2,1)S(1)}, bf16[520,256]{1,0:T(8,128)(2,1)S(1)}, u32[]{:S(2)}, u32[]{:S(2)}) %collective-permute-start.5) | collective-permute-done | bytes 266272 | tf_op jit(solution)/shard_map/ppermute | solution.py:291
  34.6 2.9 %last.3 = (f32[136,1024]{1,0:T(8,128)S(1)}, f32[136,1024]{1,0:T(8,128)S(1)}) custom-call(bf16[2048,256]{1,0:T(8,128)(2,1)S(1)} %copy-done.1, f32[2048,128]{1,0:T(8,128)S(1)} %get-tuple-element.18.total_in, f32[2048,256]{1,0:T(8,128)S(1)} %get-tuple-element.19.weighted_in, bf16[520,256]{1,0:T(8,128)(2,1)S(1)} %collective-permute-done.3.refs_0_, ...), custom_call_target="tpu_custom_call" | custom-call | flops 1610612736 | bytes 6291456 | tf_op jit(solution)/shard_map/last/pallas_call | solution.py:204
  37.5 0.1 collective-permute-start.8
  37.6 2.9 %last.2 = (f32[136,1024]{1,0:T(8,128)S(1)}, f32[136,1024]{1,0:T(8,128)S(1)}) custom-call(bf16[2048,256]{1,0:T(8,128)(2,1)S(1)} %copy-done.1, f32[2048,128]{1,0:T(8,128)S(1)} %get-tuple-element.18.total_in, f32[2048,256]{1,0:T(8,128)S(1)} %get-tuple-element.19.weighted_in, bf16[520,256]{1,0:T(8,128)(2,1)S(1)} %collective-permute-done.3.refs_0_, ...), custom_call_target="tpu_custom_call" | custom-call | flops 1610612736 | bytes 6291456 | tf_op jit(solution)/shard_map/last/pallas_call | solution.py:204
  40.6 0.0 copy-start.3
  40.6 0.6 %collective-permute-start.6 = (f32[136,1024]{1,0:T(8,128)S(1)}, f32[136,1024]{1,0:T(8,128)S(1)}, u32[]{:S(2)}, u32[]{:S(2)}) collective-permute-start(f32[136,1024]{1,0:T(8,128)S(1)} %get-tuple-element.21), channel_id=1, source_target_pairs={{0,1},{1,0},{2,3},{3,2},{4,5},{5,4},{6,7},{7,6},{8,9},{9,8},{10,11... | collective-permute-start | bytes 1671176 | tf_op jit(solution)/shard_map/ppermute | solution.py:291
  41.2 0.0 collective-permute-done.8.came_ref
  41.2 0.1 join.3
  41.2 1.2 %collective-permute-start.9 = (bf16[72,1024]{1,0:T(8,128)(2,1)S(1)}, bf16[72,1024]{1,0:T(8,128)(2,1)S(1)}, u32[]{:S(2)}, u32[]{:S(2)}) collective-permute-start(bf16[72,1024]{1,0:T(8,128)(2,1)S(1)} %get-tuple-element.27), channel_id=1, source_target_pairs={{0,2},{1,3},{2,0},{3,1},{4,6},{5,7},{6,4},{7,5},{8,10},{9,11},{10,... | collective-permute-start | bytes 442376 | tf_op jit(solution)/shard_map/ppermute | solution.py:291
  42.5 0.3 collective-permute-done.6.came_ref
  42.7 0.1 join.2
  42.8 1.2 %collective-permute-start.7 = (bf16[72,1024]{1,0:T(8,128)(2,1)S(1)}, bf16[72,1024]{1,0:T(8,128)(2,1)S(1)}, u32[]{:S(2)}, u32[]{:S(2)}) collective-permute-start(bf16[72,1024]{1,0:T(8,128)(2,1)S(1)} %get-tuple-element.23), channel_id=1, source_target_pairs={{0,2},{1,3},{2,0},{3,1},{4,6},{5,7},{6,4},{7,5},{8,10},{9,11},{10,... | collective-permute-start | bytes 442376 | tf_op jit(solution)/shard_map/ppermute | solution.py:291
  44.1 4.0 %collective-permute-done.9.refs_3_ = bf16[72,1024]{1,0:T(8,128)(2,1)S(1)} collective-permute-done((bf16[72,1024]{1,0:T(8,128)(2,1)S(1)}, bf16[72,1024]{1,0:T(8,128)(2,1)S(1)}, u32[]{:S(2)}, u32[]{:S(2)}) %collective-permute-start.9) | collective-permute-done | bytes 147488 | tf_op jit(solution)/shard_map/ppermute | solution.py:291
  48.0 2.2 %collective-permute-done.7.refs_1_ = bf16[72,1024]{1,0:T(8,128)(2,1)S(1)} collective-permute-done((bf16[72,1024]{1,0:T(8,128)(2,1)S(1)}, bf16[72,1024]{1,0:T(8,128)(2,1)S(1)}, u32[]{:S(2)}, u32[]{:S(2)}) %collective-permute-start.7) | collective-permute-done | bytes 147488 | tf_op jit(solution)/shard_map/ppermute | solution.py:291
  50.3 0.0 copy-done.3
  50.3 0.9 %finish.1 = (f32[1,2048]{1,0:T(1,128)}, f32[64,2048]{1,0:T(8,128)}) custom-call(s32[1]{0:T(128)S(6)} %copy.5.counts_ref, s32[1,2048]{1,0:T(1,128)S(1)} %bitcast.5, f32[72,1024]{1,0:T(8,128)S(1)} %get-tuple-element.22.refs_0_, bf16[72,1024]{1,0:T(8,128)(2,1)S(1)} %collective-permute-done.7.refs_1_, f32[72,1024]{1,0:T(8,128)S(1)} %get-tuple-element.26.refs_2_, ...), custom_call_target="tpu_custom_call" | custom-call | tf_op jit(solution)/shard_map/finish/pallas_call | solution.py:263
Async XLA Ops:
  1.3 1.2 %copy-start = (bf16[2048,256]{1,0:T(8,128)(2,1)S(1)}, bf16[2048,256]{1,0:T(8,128)(2,1)}, u32[]{:S(2)}) copy-start(bf16[2048,256]{1,0:T(8,128)(2,1)} %query_ref.7) | copy-start | bytes 3145732
  2.5 0.7 %copy-start.2 = (s32[2048]{0:T(1024)S(1)}, s32[2048]{0:T(1024)}, u32[]{:S(2)}) copy-start(s32[2048]{0:T(1024)} %param.5) | copy-start | bytes 24580
  4.3 14.8 %collective-permute-start = (bf16[520,256]{1,0:T(8,128)(2,1)S(1)}, bf16[520,256]{1,0:T(8,128)(2,1)S(1)}, u32[]{:S(2)}, u32[]{:S(2)}) collective-permute-start(bf16[520,256]{1,0:T(8,128)(2,1)S(1)} %pack.1.message_ref), channel_id=1, source_target_pairs={{0,248},{1,249},{2,250},{3,251},{4,12},{5,13},{6,14},{7,15},{8,0},... | collective-permute-start | bytes 798728 | tf_op jit(solution)/shard_map/ppermute | solution.py:291
  6.3 16.0 %collective-permute-start.1 = (bf16[520,256]{1,0:T(8,128)(2,1)S(1)}, bf16[520,256]{1,0:T(8,128)(2,1)S(1)}, u32[]{:S(2)}, u32[]{:S(2)}) collective-permute-start(bf16[520,256]{1,0:T(8,128)(2,1)S(1)} %pack.1.message_ref), channel_id=1, source_target_pairs={{0,6},{1,7},{2,4},{3,5},{4,2},{5,3},{6,0},{7,1},{8,14},{9,15},{10,... | collective-permute-start | bytes 798728 | tf_op jit(solution)/shard_map/ppermute | solution.py:291
  13.2 9.4 %collective-permute-start.2 = (bf16[520,256]{1,0:T(8,128)(2,1)S(1)}, bf16[520,256]{1,0:T(8,128)(2,1)S(1)}, u32[]{:S(2)}, u32[]{:S(2)}) collective-permute-start(bf16[520,256]{1,0:T(8,128)(2,1)S(1)} %pack.1.message_ref), channel_id=1, source_target_pairs={{0,8},{1,9},{2,10},{3,11},{4,252},{5,253},{6,254},{7,255},{8,16},{... | collective-permute-start | bytes 798728 | tf_op jit(solution)/shard_map/ppermute | solution.py:291
  14.2 1.2 %copy-start.1 = (bf16[2048,256]{1,0:T(8,128)(2,1)S(1)}, bf16[2048,256]{1,0:T(8,128)(2,1)}, u32[]{:S(2)}) copy-start(bf16[2048,256]{1,0:T(8,128)(2,1)} %query_ref.7) | copy-start | bytes 3145732
  19.1 10.2 %collective-permute-start.3 = (bf16[520,256]{1,0:T(8,128)(2,1)S(1)}, bf16[520,256]{1,0:T(8,128)(2,1)S(1)}, u32[]{:S(2)}, u32[]{:S(2)}) collective-permute-start(bf16[520,256]{1,0:T(8,128)(2,1)S(1)} %collective-permute-done.refs_0_), channel_id=1, source_target_pairs={{0,254},{1,255},{2,252},{3,253},{4,10},{5,11},{6,8},{7,9},{8,6},{9... | collective-permute-start | bytes 798728 | tf_op jit(solution)/shard_map/ppermute | solution.py:291
  19.1 14.1 %collective-permute-start.4 = (bf16[520,256]{1,0:T(8,128)(2,1)S(1)}, bf16[520,256]{1,0:T(8,128)(2,1)S(1)}, u32[]{:S(2)}, u32[]{:S(2)}) collective-permute-start(bf16[520,256]{1,0:T(8,128)(2,1)S(1)} %collective-permute-done.refs_0_), channel_id=1, source_target_pairs={{0,6},{1,7},{2,4},{3,5},{4,2},{5,3},{6,0},{7,1},{8,14},{9,15},{10,... | collective-permute-start | bytes 798728 | tf_op jit(solution)/shard_map/ppermute | solution.py:291
  22.3 12.4 %collective-permute-start.5 = (bf16[520,256]{1,0:T(8,128)(2,1)S(1)}, bf16[520,256]{1,0:T(8,128)(2,1)S(1)}, u32[]{:S(2)}, u32[]{:S(2)}) collective-permute-start(bf16[520,256]{1,0:T(8,128)(2,1)S(1)} %collective-permute-done.1.refs_1_), channel_id=1, source_target_pairs={{0,248},{1,249},{2,250},{3,251},{4,12},{5,13},{6,14},{7,15},{8,0},... | collective-permute-start | bytes 798728 | tf_op jit(solution)/shard_map/ppermute | solution.py:291
  37.5 3.6 %collective-permute-start.8 = (f32[136,1024]{1,0:T(8,128)S(1)}, f32[136,1024]{1,0:T(8,128)S(1)}, u32[]{:S(2)}, u32[]{:S(2)}) collective-permute-start(f32[136,1024]{1,0:T(8,128)S(1)} %get-tuple-element.25), channel_id=1, source_target_pairs={{0,1},{1,0},{2,3},{3,2},{4,5},{5,4},{6,7},{7,6},{8,9},{9,8},{10,11... | collective-permute-start | bytes 1671176 | tf_op jit(solution)/shard_map/ppermute | solution.py:291
  40.6 9.7 %copy-start.3 = (s32[2048]{0:T(1024)S(1)}, s32[2048]{0:T(1024)}, u32[]{:S(2)}) copy-start(s32[2048]{0:T(1024)} %param.5) | copy-start | bytes 24580
  40.6 2.1 %collective-permute-start.6 = (f32[136,1024]{1,0:T(8,128)S(1)}, f32[136,1024]{1,0:T(8,128)S(1)}, u32[]{:S(2)}, u32[]{:S(2)}) collective-permute-start(f32[136,1024]{1,0:T(8,128)S(1)} %get-tuple-element.21), channel_id=1, source_target_pairs={{0,1},{1,0},{2,3},{3,2},{4,5},{5,4},{6,7},{7,6},{8,9},{9,8},{10,11... | collective-permute-start | bytes 1671176 | tf_op jit(solution)/shard_map/ppermute | solution.py:291
  41.2 6.8 %collective-permute-start.9 = (bf16[72,1024]{1,0:T(8,128)(2,1)S(1)}, bf16[72,1024]{1,0:T(8,128)(2,1)S(1)}, u32[]{:S(2)}, u32[]{:S(2)}) collective-permute-start(bf16[72,1024]{1,0:T(8,128)(2,1)S(1)} %get-tuple-element.27), channel_id=1, source_target_pairs={{0,2},{1,3},{2,0},{3,1},{4,6},{5,7},{6,4},{7,5},{8,10},{9,11},{10,... | collective-permute-start | bytes 442376 | tf_op jit(solution)/shard_map/ppermute | solution.py:291
  42.8 7.4 %collective-permute-start.7 = (bf16[72,1024]{1,0:T(8,128)(2,1)S(1)}, bf16[72,1024]{1,0:T(8,128)(2,1)S(1)}, u32[]{:S(2)}, u32[]{:S(2)}) collective-permute-start(bf16[72,1024]{1,0:T(8,128)(2,1)S(1)} %get-tuple-element.23), channel_id=1, source_target_pairs={{0,2},{1,3},{2,0},{3,1},{4,6},{5,7},{6,4},{7,5},{8,10},{9,11},{10,... | collective-permute-start | bytes 442376 | tf_op jit(solution)/shard_map/ppermute | solution.py:291
